TPU v7x, 32 devices: a whole 2x2x4 slice. The times are simulated.
32 devices in a mesh: ctx: 8 (over z, x), tp: 4 (over y, core).
Axes of the slice: x: 2, y: 2, z: 4, core: 2. Of those that a mesh axis runs over, the one named last changes fastest.
Arguments:
- hidden: bfloat16 [2048, 2048], P(('ctx', 'tp')), may hold values from -14 to 14
- in_weight: bfloat16 [2048, 2, 4096], P(None, None, 'tp'), may hold values from -0.125 to 0.125
- step_weight: bfloat16 [2048, 64], P(None, 'tp'), may hold values from -0.125 to 0.125
- group_weight: bfloat16 [256, 4, 2048], P('tp'), may hold values from -0.125 to 0.125
- conv_inner: float32 [4, 4096], P(None, 'tp'), may hold values from -3 to 3
- inner_bias: float32 [4096], P('tp'), may hold values from -2.5 to 2.5
- conv_group: float32 [4, 1024], replicated, may hold values from -3 to 3
- group_bias: float32 [1024], replicated, may hold values from -2.5 to 2.5
- step_bias: float32 [64], P('tp'), may hold values from -9.5 to 0
- log_rate: float32 [64], P('tp'), may hold values from -2.5 to -0.5
- skip_weight: float32 [64], P('tp'), may hold values from 0.25 to 1
- norm_gain: float32 [4096], P('tp'), may hold values from 0.1 to 1.9
- out_weight: bfloat16 [4096, 2048], P('tp'), may hold values from -0.09375 to 0.09375
Outputs:
- mixed: bfloat16 [2048, 2048], P(('ctx', 'tp'))
All inputs are finite; a program needn't handle non-finite values.
Results may differ from a plain program's by a relative error of at most 0.024.
Values may be sent and summed in bfloat16 or wider, within the bound.
A program may use at most 64 MiB of HBM per device.

v0:
```python
import jax
import jax.numpy as jnp
from jax import lax
from jax.sharding import PartitionSpec as P

HEADS = 64
HEAD_DIM = 64
STATE = 128
GROUPS = 4
BLOCK = 256
KERNEL = 4


def shifted(x, axis, by):
    peers = lax.axis_size(axis)
    pairs = [(i, i + by) for i in range(peers) if 0 <= i + by < peers]
    return lax.ppermute(x, axis, pairs)


def entering(x, axis, combine, identity):
    peers, place = (lax.axis_size(axis), lax.axis_index(axis))
    everything = jax.tree.map(lambda part: lax.all_gather(part, axis), x)
    start = jax.tree.map(
        lambda part, zero: jnp.broadcast_to(jnp.asarray(zero, part.dtype), part.shape), x, identity
    )

    def turn(k, before):
        reached = k < place
        new = combine(before, jax.tree.map(lambda part: part[k], everything))
        return jax.tree.map(lambda a, b: jnp.where(reached, a, b), new, before)

    return lax.fori_loop(0, peers, turn, start)


def causal_conv(prior_rows, raw_rows, conv_weight, conv_bias):
    joined = jnp.concatenate([prior_rows, raw_rows], axis=0).astype(jnp.float32)
    length = raw_rows.shape[0]
    running = jnp.broadcast_to(conv_bias[None, :], raw_rows.shape)
    for offset in range(conv_weight.shape[0]):
        running = running + conv_weight[offset][None, :] * joined[offset : offset + length]
    return jax.nn.silu(running).astype(jnp.bfloat16)


def combine_states(earlier, latter):
    return (earlier[0] * latter[0], latter[0][:, None, None] * earlier[1] + latter[1])


def body(
    hidden,
    in_weight,
    step_weight,
    group_weight,
    conv_inner,
    inner_bias,
    conv_group,
    group_bias,
    step_bias,
    log_rate,
    skip_weight,
    norm_gain,
    out_weight,
):
    heads_dev = log_rate.shape[0]
    inner_dev = in_weight.shape[2]
    group_cols = 2 * STATE
    group_index = lax.axis_index("tp") * heads_dev // (HEADS // GROUPS)
    zx_weight = in_weight.reshape(in_weight.shape[0], 2 * inner_dev)
    full_weight = lax.all_gather(group_weight, "tp", axis=0, tiled=True)
    map_weight = lax.dynamic_slice_in_dim(full_weight, group_index, 1, 1)[:, 0, :]
    shard_rows = lax.all_gather(hidden, "tp", axis=0, tiled=True)
    projected = jnp.concatenate(
        [
            jnp.dot(shard_rows, zx_weight, preferred_element_type=jnp.float32),
            lax.dot_general(
                shard_rows, map_weight, (((1,), (1,)), ((), ())), preferred_element_type=jnp.float32
            ),
            jnp.dot(shard_rows, step_weight, preferred_element_type=jnp.float32),
        ],
        axis=1,
    ).astype(jnp.bfloat16)
    gate_raw = projected[:, :inner_dev]
    inner_raw = projected[:, inner_dev : 2 * inner_dev]
    map_part = projected[:, 2 * inner_dev : projected.shape[1] - heads_dev]
    step_raw = projected[:, projected.shape[1] - heads_dev :]
    border_rows = KERNEL - 1
    length = inner_raw.shape[0]
    inner_prior, map_prior = shifted(
        (inner_raw[length - border_rows :], map_part[length - border_rows :]), "ctx", 1
    )
    x_conv = causal_conv(inner_prior, inner_raw, conv_inner, inner_bias)
    own_taps = lax.dynamic_slice_in_dim(conv_group, group_index * group_cols, group_cols, 1)
    own_bias = lax.dynamic_slice_in_dim(group_bias, group_index * group_cols, group_cols, 0)
    maps = causal_conv(map_prior, map_part, own_taps, own_bias)
    step_size = jax.nn.softplus(step_raw.astype(jnp.float32) + step_bias[None, :])
    decay_rate = -jnp.exp(log_rate)
    blocks = length // BLOCK
    x_blocks = x_conv.reshape(blocks, BLOCK, heads_dev, HEAD_DIM)
    input_map = maps[:, :STATE].reshape(blocks, BLOCK, STATE)
    output_map = maps[:, STATE:].reshape(blocks, BLOCK, STATE)
    step_blocks = jnp.swapaxes(step_size.reshape(blocks, BLOCK, heads_dev), 1, 2)
    cumulative = jnp.cumsum(step_blocks * decay_rate[None, :, None], axis=2)
    scores = jnp.einsum("kin,kjn->kij", output_map, input_map, preferred_element_type=jnp.float32)
    causal = jnp.arange(BLOCK)[:, None] >= jnp.arange(BLOCK)[None, :]
    exponent = jnp.where(causal, cumulative[..., :, None] - cumulative[..., None, :], -jnp.inf)
    mixing = (scores[:, None] * jnp.exp(exponent) * step_blocks[..., None, :]).astype(jnp.bfloat16)
    within = jnp.einsum("khij,kjhp->kihp", mixing, x_blocks, preferred_element_type=jnp.float32)
    weight = jnp.exp(cumulative[..., BLOCK - 1 :] - cumulative) * step_blocks
    x_float = x_blocks.astype(jnp.float32)
    weighted = (x_float * jnp.swapaxes(weight, 1, 2)[..., None]).astype(jnp.bfloat16)
    block_state = jnp.einsum(
        "kjhp,kjn->khpn", weighted, input_map, preferred_element_type=jnp.float32
    )
    block_decay = jnp.exp(cumulative[..., BLOCK - 1])

    def advance(carry, item):
        running, product = carry
        block_stop_index, state_here = item
        return (
            (block_stop_index[:, None, None] * running + state_here, product * block_stop_index),
            (running, product),
        )

    empty_state = jnp.zeros((heads_dev, HEAD_DIM, STATE), jnp.float32)
    (dev_state, dev_decay), (local_starts, prefixes) = lax.scan(
        advance, (empty_state, jnp.ones((heads_dev,), jnp.float32)), (block_decay, block_state)
    )
    decay_in, incoming = entering(
        (dev_decay, dev_state),
        "ctx",
        combine_states,
        (jnp.ones_like(dev_decay), jnp.zeros_like(dev_state)),
    )
    starting = local_starts + prefixes[:, :, None, None] * incoming[None]
    carried = jnp.einsum(
        "kin,khpn->kihp",
        output_map,
        starting.astype(jnp.bfloat16),
        preferred_element_type=jnp.float32,
    )
    carried = carried * jnp.swapaxes(jnp.exp(cumulative), 1, 2)[..., None]
    result_heads = within + carried + skip_weight[None, None, :, None] * x_float
    result_heads = result_heads.reshape(length, inner_dev)
    gated = result_heads * jax.nn.silu(gate_raw.astype(jnp.float32))
    squares = jnp.sum(gated * gated, axis=1)
    own_slot = (jnp.arange(GROUPS) == group_index)[:, None]
    group_sums = lax.psum(jnp.where(own_slot, squares[None, :], 0.0), "tp")
    own_total = jnp.sum(jnp.where(own_slot, group_sums, 0.0), axis=0)
    inverse = lax.rsqrt(own_total / (HEADS * HEAD_DIM // GROUPS) + 1e-05)
    normed = (gated * inverse[:, None] * norm_gain[None, :]).astype(jnp.bfloat16)
    mixed = lax.psum_scatter(
        jnp.dot(normed, out_weight, preferred_element_type=jnp.float32),
        "tp",
        scatter_dimension=0,
        tiled=True,
    )
    return mixed.astype(jnp.bfloat16)


def solution(mesh):
    placed = (
        P(("ctx", "tp"), None),
        P(None, None, "tp"),
        P(None, "tp"),
        P("tp", None, None),
        P(None, "tp"),
        P("tp"),
        P(),
        P(),
        P("tp"),
        P("tp"),
        P("tp"),
        P("tp"),
        P("tp", None),
    )
    return jax.shard_map(
        body, mesh=mesh, in_specs=placed, out_specs=P(("ctx", "tp"), None), check_vma=False
    )
```

profile of v0, /device:TPU:0, one launch (start us, length us, event | category | flops | bytes accessed | tf_op | source)
XLA Modules:
  0.0 214.4 jit_solution(5556542507747364428)
XLA Ops:
  6.5 0.7 all-gather.6.cloned.1.call-update
  7.3 0.0 all-gather.8.cloned.1.call-start
  7.3 2.8 %copy.55 = bf16[64,4,2048]{2,0,1:T(8,128)(2,1)} copy(bf16[64,4,2048]{2,1,0:T(4,128)(2,1)} %param.18) | data formatting | bytes 2097152 | tf_op args[3]
  10.1 0.0 all-gather.8.cloned.1.call-update
  10.1 0.0 all-gather.10.cloned.1.call-start
  10.2 0.0 copy-start.8
  10.2 0.0 copy-start.9
  10.2 10.1 %copy.70 = bf16[256,8,2,1024]{3,1,2,0:T(8,128)(2,1)} copy(bf16[256,8,2,1024]{3,2,1,0:T(2,128)(2,1)} %bitcast.92) | data formatting | bytes 16777216
  20.4 1.3 dynamic_slice.29
  21.7 1.5 constant_dynamic-slice_fusion
  23.2 5.1 %all-gather.6.cloned.1.call-done = bf16[256,2048]{1,0:T(8,128)(2,1)} async-done(((bf16[64,2048]{1,0:T(8,128)(2,1)}), bf16[256,2048]{1,0:T(8,128)(2,1)}) %all-gather.6.cloned.1.call-update) | async-done | bytes 1048592 | tf_op jit(solution)/shard_map/all_gather | solution.py:70
  28.4 1.7 bitcast_multiply_fusion.1
  30.1 0.0 copy-start.3
  30.1 0.1 copy.57
  30.1 0.6 reduce-window.6
  30.7 0.1 copy.61
  30.8 0.2 slice_reduce_fusion
  31.0 6.1 %convolution_convert_fusion = bf16[256,2048]{1,0:T(8,128)(2,1)S(1)} fusion(bf16[256,2048]{1,0:T(8,128)(2,1)} %all-gather.6.cloned.1.call-done, bf16[2048,2048]{1,0:T(8,128)(2,1)} %bitcast.93), kind=kOutput, calls=%fused_computation.4 | convolution fusion | flops 2148007936 | bytes 10485760 | tf_op jit(solution)/shard_map/dot_general | solution.py:73
  37.1 3.4 %collective-permute-start = (bf16[3,1024]{1,0:T(4,128)(2,1)S(1)}, bf16[3,1024]{1,0:T(4,128)(2,1)S(1)}, u32[]{:S(2)}, u32[]{:S(2)}) collective-permute-start(bf16[3,1024]{1,0:T(4,128)(2,1)S(1)} %slice.112), channel_id=1, source_target_pairs={{0,4},{4,8},{8,12},{12,16},{16,20},{20,24},{24,28},{1,5},{5,9},{9,... | collective-permute-start | bytes 18440 | tf_op jit(solution)/shard_map/ppermute | solution.py:17
  40.5 0.6 slice_bitcast_fusion.1
  41.1 0.5 exponential_multiply_fusion
  41.7 0.1 copy.62
  41.8 0.1 mul.283
  41.9 0.3 copy.63
  42.2 0.1 maximum_convert_fusion
  42.4 22.1 %all-gather.8.cloned.1.call-done = bf16[256,4,2048]{2,0,1:T(8,128)(2,1)} async-done(((bf16[64,4,2048]{2,0,1:T(8,128)(2,1)}), bf16[256,4,2048]{2,0,1:T(8,128)(2,1)}) %all-gather.8.cloned.1.call-update) | async-done | bytes 4194320 | tf_op jit(solution)/shard_map/all_gather | solution.py:68
  64.5 2.0 fusion.12
  66.5 0.6 slice.118
  67.1 3.9 %collective-permute-start.1 = (bf16[3,256]{1,0:T(4,128)(2,1)}, bf16[3,256]{1,0:T(4,128)(2,1)}, u32[]{:S(2)}, u32[]{:S(2)}) collective-permute-start(bf16[3,256]{1,0:T(4,128)(2,1)} %slice.118), channel_id=1, source_target_pairs={{0,4},{4,8},{8,12},{12,16},{16,20},{20,24},{24,28},{1,5},{5,9},{9,... | collective-permute-start | bytes 4616 | tf_op jit(solution)/shard_map/ppermute | solution.py:17
  71.0 1.4 multiply_convert_fusion.9
  72.4 0.2 copy.64
  72.6 0.7 maximum_convert_fusion.1
  73.3 0.9 multiply_convert_fusion.12
  74.2 1.7 convolution_add_fusion
  75.9 0.0 all-gather.10.cloned.1.call-update
  75.9 0.0 reduce-scatter.2.cloned.1.call-start
  76.1 0.1 copy.65
  76.1 0.1 copy.69
  76.2 0.1 copy.60
  76.3 20.9 %all-gather = f32[8,16,1]{1,2,0:T(1,128)S(1)} all-gather(f32[1,16,1]{1,2,0:T(1,128)S(1)} %copy-done.6), channel_id=2, replica_groups=mesh['ctx'=8,'tp'=4] {'ctx'}, dimensions={0}, use_global_device_ids=true | all-gather | bytes 576 | tf_op jit(solution)/shard_map/all_gather | solution.py:22
  97.2 0.2 copy.66
  97.4 1.0 copy.54
  98.4 0.2 fusion.37
  98.6 51.1 %all-gather.10.cloned.1.call-done = f32[128,64,128]{2,1,0:T(8,128)} async-done(((f32[16,64,128]{2,1,0:T(8,128)}), f32[128,64,128]{2,1,0:T(8,128)}) %all-gather.10.cloned.1.call-update) | async-done | bytes 4194320 | tf_op jit(solution)/shard_map/all_gather | solution.py:22
  149.7 9.7 %while.9 = (s32[]{:T(128)}, f32[16,64,128]{2,1,0:T(8,128)S(1)}, s32[]{:T(128)}, f32[8,16]{1,0:T(8,128)S(1)}, f32[8,16,64,128]{3,2,1,0:T(8,128)}, /*index=5*/s32[]{:T(128)}, s32[]{:T(128)}) while((s32[]{:T(128)}, f32[16,64,128]{2,1,0:T(8,128)S(1)}, s32[]{:T(128)}, f32[8,16]{1,0:T(8,128)S(1)}, f32[8,16,64,128]{3,2,1,0:T(8,128)}, ...), condition=%wide.region_3.4_spmd.clone, body=%wide.region_2.3_spmd.clone.sunk | while | flops 524292 | bytes 1573161 | solution.py:32
  149.7 1.2 fusion.54
  150.9 1.2 fusion.54
  152.1 1.2 fusion.54
  153.3 1.2 fusion.54
  154.5 1.2 fusion.54
  155.8 1.2 fusion.54
  157.0 1.2 fusion.54
  158.2 1.2 fusion.54
  159.4 0.3 fusion.9
  159.7 3.4 %fusion.11 = f32[1,256,16,64]{1,3,2,0:T(8,128)} fusion(f32[1,256,16,64]{1,3,2,0:T(8,128)S(1)} %fusion.9, bf16[256,16,64]{0,2,1:T(8,128)(2,1)} %bitcast.99, f32[16,256]{1,0:T(8,128)S(1)} %copy.60, f32[16,256]{1,0:T(8,128)S(1)} %bitcast_add_fusion.2, f32[256,256]{1,0:T(8,128)S(1)} %fusion.37, pred[256,256]{1,0:T(8,128)(4,1)S(1)} %iota_compare_fusion, ...), kind=kOutput, calls=%fused_computation.16 | convolution fusion | flops 140247040 | bytes 4030528 | tf_op jit(solution)/shard_map/khij,kjhp->kihp/dot_general | solution.py:106
  163.1 1.6 copy.67
  164.7 0.4 multiply_reduce_fusion
  165.1 0.1 broadcast_select_fusion
  165.2 5.6 %psum.7 = f32[4,256]{1,0:T(4,128)S(1)} all-reduce(f32[4,256]{1,0:T(4,128)S(1)} %broadcast_select_fusion), channel_id=1, replica_groups=mesh['ctx'=8,'tp'=4] {'tp'}, use_global_device_ids=true, to_apply=%region_5.6 | all-reduce | flops 1024 | bytes 8192 | tf_op jit(solution)/shard_map/psum | solution.py:146
  170.8 0.1 select_reduce_fusion
  170.9 5.0 %fusion.25 = f32[256,2048]{1,0:T(8,128)} fusion(bf16[1024,2048]{1,0:T(8,128)(2,1)} %param.27, f32[1024]{0:T(1024)S(1)} %copy-done.7, f32[256]{0:T(256)S(1)} %add_rsqrt_fusion, f32[256,1024]{1,0:T(8,128)S(1)} %copy.67, bf16[256,2048]{1,0:T(8,128)(2,1)S(1)} %copy-done.2), kind=kOutput, calls=%fused_computation.44 | convolution fusion | flops 1076101120 | bytes 7869440 | tf_op jit(solution)/shard_map/dot_general | solution.py:151
  175.9 0.0 reduce-scatter.2.cloned.1.call-update
  176.0 30.1 %reduce-scatter.2.cloned.1.call-done = f32[64,2048]{1,0:T(8,128)} async-done(((f32[256,2048]{1,0:T(8,128)}), f32[64,2048]{1,0:T(8,128)}) %reduce-scatter.2.cloned.1.call-update) | async-done | bytes 524304 | tf_op jit(solution)/shard_map/reduce_scatter | solution.py:150
  206.1 1.8 convert_element_type.77
  (45 shorter events, 0.3 us)
Async XLA Ops:
  6.5 21.8 %copy-start = (bf16[2048,16]{0,1:T(8,128)(2,1)S(1)}, bf16[2048,16]{0,1:T(8,128)(2,1)}, u32[]{:S(2)}) copy-start(bf16[2048,16]{0,1:T(8,128)(2,1)} %param.17) | copy-start | bytes 196612
  6.5 21.8 %all-gather.6.cloned.1.call-start = ((), (), s32[]{:S(2)}) async-start(), calls=%async_computation.1 | async-start | bytes 1310720 | tf_op jit(solution)/shard_map/all_gather | solution.py:70
  7.3 57.2 %all-gather.8.cloned.1.call-start = ((), (), s32[]{:S(2)}) async-start(), calls=%async_computation.2 | async-start | bytes 5242880 | tf_op jit(solution)/shard_map/all_gather | solution.py:68
  10.1 139.6 %all-gather.10.cloned.1.call-start = ((), (), s32[]{:S(2)}) async-start(), calls=%async_computation.4 | async-start | bytes 4718592 | tf_op jit(solution)/shard_map/all_gather | solution.py:22
  10.2 13.0 %copy-start.8 = (f32[16]{0:T(128)S(1)}, f32[16]{0:T(128)}, u32[]{:S(2)}) copy-start(f32[16]{0:T(128)} %param.24) | copy-start | bytes 196
  10.2 13.0 %copy-start.5 = (f32[4,1024]{1,0:T(4,128)S(1)}, f32[4,1024]{1,0:T(4,128)}, u32[]{:S(2)}) copy-start(f32[4,1024]{1,0:T(4,128)} %param.19) | copy-start | bytes 49156
  10.2 18.2 %copy-start.9 = (f32[16]{0:T(128)S(1)}, f32[16]{0:T(128)}, u32[]{:S(2)}) copy-start(f32[16]{0:T(128)} %param.23) | copy-start | bytes 196
  30.1 11.1 %copy-start.3 = (f32[256,16]{1,0:T(8,128)}, f32[256,16]{1,0:T(8,128)S(1)}, u32[]{:S(2)}) copy-start(f32[256,16]{1,0:T(8,128)S(1)} %get-tuple-element.164) | copy-start | bytes 49156
  37.1 4.6 %copy-start.1 = (bf16[256,2048]{1,0:T(8,128)(2,1)}, bf16[256,2048]{1,0:T(8,128)(2,1)S(1)}, u32[]{:S(2)}) copy-start(bf16[256,2048]{1,0:T(8,128)(2,1)S(1)} %convolution_convert_fusion) | copy-start | bytes 3145732
  37.1 5.1 %collective-permute-start = (bf16[3,1024]{1,0:T(4,128)(2,1)S(1)}, bf16[3,1024]{1,0:T(4,128)(2,1)S(1)}, u32[]{:S(2)}, u32[]{:S(2)}) collective-permute-start(bf16[3,1024]{1,0:T(4,128)(2,1)S(1)} %slice.112), channel_id=1, source_target_pairs={{0,4},{4,8},{8,12},{12,16},{16,20},{20,24},{24,28},{1,5},{5,9},{9,... | collective-permute-start | bytes 18440 | tf_op jit(solution)/shard_map/ppermute | solution.py:17
  67.1 5.6 %collective-permute-start.1 = (bf16[3,256]{1,0:T(4,128)(2,1)}, bf16[3,256]{1,0:T(4,128)(2,1)}, u32[]{:S(2)}, u32[]{:S(2)}) collective-permute-start(bf16[3,256]{1,0:T(4,128)(2,1)} %slice.118), channel_id=1, source_target_pairs={{0,4},{4,8},{8,12},{12,16},{16,20},{20,24},{24,28},{1,5},{5,9},{9,... | collective-permute-start | bytes 4616 | tf_op jit(solution)/shard_map/ppermute | solution.py:17
  72.4 3.8 %copy-start.4 = (f32[256,16]{1,0:T(8,128)S(1)}, f32[256,16]{1,0:T(8,128)}, u32[]{:S(2)}) copy-start(f32[256,16]{1,0:T(8,128)} %copy-done.3) | copy-start | bytes 49156
  72.4 3.9 %copy-start.6 = (f32[1,16,1]{1,2,0:T(1,128)S(1)}, f32[1,16,1]{1,2,0:T(1,128)}, u32[]{:S(2)}) copy-start(f32[1,16,1]{1,2,0:T(1,128)} %get-tuple-element.154) | copy-start | bytes 196
  75.9 130.2 %reduce-scatter.2.cloned.1.call-start = ((), (), s32[]{:S(2)}) async-start(), calls=%async_computation.3 | async-start | bytes 2621440 | tf_op jit(solution)/shard_map/reduce_scatter | solution.py:150
  149.7 10.0 %copy-start.10 = (f32[16]{0:T(128)S(1)}, f32[16]{0:T(128)}, u32[]{:S(2)}) copy-start(f32[16]{0:T(128)} %param.25) | copy-start | bytes 196
  159.7 5.0 %copy-start.2 = (bf16[256,2048]{1,0:T(8,128)(2,1)S(1)}, bf16[256,2048]{1,0:T(8,128)(2,1)}, u32[]{:S(2)}) copy-start(bf16[256,2048]{1,0:T(8,128)(2,1)} %copy-done.1) | copy-start | bytes 3145732
  159.7 11.2 %copy-start.7 = (f32[1024]{0:T(1024)S(1)}, f32[1024]{0:T(1024)}, u32[]{:S(2)}) copy-start(f32[1024]{0:T(1024)} %param.26) | copy-start | bytes 12292
Sparse Core Ops, SparseCore 0:
  8.9 19.4 all-gather.5
  29.9 34.4 all-gather.7
  76.0 73.5 all-gather.9
  176.1 29.9 reduce-scatter.1
where the time goes:
time: 215 us; the launch traced here: 214 us
  waiting for transfers between devices  109 us (51%)
  blocking collectives  26.5 us (12%)
  local copies, waits for them, and re-layouts  21.1 us (10%)
  matrix products  20.4 us (9%)
  other arithmetic  16.1 us (7%)
  between operations  13.5 us (6%)
  starting transfers between devices  7.41 us (3%)
    all_gather x1, waiting for transfers between devices, entering(): everything = jax.tree.map(lambda part: lax.all_gather(part, axis), x)  51.1 us
    reduce_scatter x1, waiting for transfers between devices, body(): lax.psum_scatter(jnp.dot(normed, out_weight, preferred_element_type=jnp.f...  30.1 us
    all_gather x1, waiting for transfers between devices, body(): full_weight = lax.all_gather(group_weight, 'tp', axis=0, tiled=True)  22.1 us
    all_gather x1, blocking collectives, entering(): everything = jax.tree.map(lambda part: lax.all_gather(part, axis), x)  20.9 us
    unnamed x24, local copies, waits for them, and re-layouts  13 us
    select_n x8, other arithmetic, turn(): return jax.tree.map(lambda a, b: jnp.where(reached, a, b), new, before)  9.38 us
    ppermute x2, starting transfers between devices, shifted(): return lax.ppermute(x, axis, pairs)  7.29 us
    dot_general x1, matrix products, body(): jnp.dot(shard_rows, zx_weight, preferred_element_type=jnp.float32)  6.05 us
  transfers between devices with their start and end apart: 6, of which 4 were waited for; matrix products, arithmetic and copies ran while one was open for 14% of the time, Pallas kernels for 0%

commit v1 on v0

v1 whole, which is shorter than its diff:
```python
import functools

import jax
import jax.numpy as jnp
from jax import lax
from jax.experimental import pallas as pl
from jax.experimental.pallas import tpu as pltpu
from jax.sharding import PartitionSpec as P

HEADS = 64
HEAD_DIM = 64
STATE = 128
GROUPS = 4
KERNEL = 4
PAD = 16
LANES = 128
F32 = jnp.float32
BF16 = jnp.bfloat16
NT = (((1,), (1,)), ((), ()))


def dot(a, b):
    return jnp.dot(a, b, preferred_element_type=F32)


def dot_nt(a, b):
    return lax.dot_general(a, b, NT, preferred_element_type=F32)


def silu(v):
    half = 0.5 * v
    return half + half * jnp.tanh(half)


def softplus(v):
    e = jnp.exp(-jnp.abs(v))
    small = e * (1.0 - e * (0.5 - e * (1.0 / 3.0)))
    return jnp.maximum(v, 0.0) + jnp.where(e < 0.01, small, jnp.log(1.0 + e))


def split_terms(a):
    hi = a.astype(BF16)
    lo = (a - hi.astype(F32)).astype(BF16)
    return jnp.concatenate([hi, lo], axis=1)


def iota(shape, dim):
    return lax.broadcasted_iota(jnp.int32, shape, dim)


def kernel(
    sizes,
    hidden, in_w, step_w, group_w, conv_inner, inner_bias, conv_group, group_bias,
    step_bias, log_rate, skip_weight, norm_gain, out_w,
    out,
    xbuf, w_vm, gw_vm, ow_vm, sw_pad, rows_pad, xeo, raw, gate_buf, map_send, map_recv,
    map_raw, x_buf, st_send, st_recv, dec_buf, dec_recv, start_out, start_buf, xt_buf, gated_buf, nbuf,
    rs_send1, rs_recv1, s_buf, rs_send2, rs_recv2, sq_send, sq_recv,
    w_sem, gw_sem, ow_sem, own_sem,
    ys_sem, yr_sem, ps_sem, pr_sem, hs_sem, hr_sem,
    ms_sem, mr_sem, ss_sem, sr_sem, ds_sem, dr_sem, bs_sem, br_sem,
    q1s_sem, q1r_sem, q2s_sem, q2r_sem, sqs_sem, sqr_sem,
):
    C, T = sizes
    Y = T // 2
    r = hidden.shape[0]
    R = r * T
    D = hidden.shape[1]
    inner = out_w.shape[0]
    heads = step_w.shape[0]
    m_dev = group_w.shape[0]
    span = T // GROUPS
    NS = st_send.shape[0]
    slice_rows = STATE // NS
    stride = C // NS
    NC = rs_send1.shape[0]
    cols = rs_send1.shape[2]
    c = lax.axis_index("ctx")
    t = lax.axis_index("tp")
    y = t // 2
    core = t % 2
    group = t // span

    def at(cc, tt):
        return {"ctx": cc, "tp": tt}

    def remote(src, dst, ssem, rsem, cc, tt):
        return pltpu.make_async_remote_copy(
            src_ref=src, dst_ref=dst, send_sem=ssem, recv_sem=rsem,
            device_id=(cc, tt), device_id_type=pl.DeviceIdType.MESH,
        )

    gws = [
        pltpu.make_async_copy(group_w.at[:, :, pl.ds(k * LANES, LANES)], gw_vm.at[k], gw_sem.at[k])
        for k in range(D // LANES)
    ]
    ws = [
        pltpu.make_async_copy(in_w.at[:, :, pl.ds(k * LANES, LANES)], w_vm.at[k], w_sem.at[k])
        for k in range(inner // LANES)
    ]
    ow = pltpu.make_async_copy(out_w, ow_vm, ow_sem)
    own = pltpu.make_async_copy(hidden, xbuf.at[pl.ds(PAD + t * r, r)], own_sem)
    own.start()
    for cp in gws:
        cp.start()
    for cp in ws:
        cp.start()
    ow.start()

    barrier = pltpu.get_barrier_semaphore()

    def greet(cc, tt):
        pl.semaphore_signal(barrier, inc=1, device_id=(cc, tt), device_id_type=pl.DeviceIdType.MESH)

    for d in range(1, T):
        greet(c, (t + d) % T)
    for d in range(1, C):
        greet((c + d) % C, t)
    has_next = jnp.logical_and(t == T - 1, c < C - 1)

    @pl.when(c > 0)
    def _():
        greet(c - 1, T - 1)

    pl.semaphore_wait(barrier, T - 1 + C - 1 + jnp.where(has_next, T, 0))

    row_of = lambda s: pl.ds(PAD + s * r, r)
    partner = y * 2 + (1 - core)
    y_copies = []
    for d in range(1, Y):
        tt = ((y + d) % Y) * 2 + core
        cp = remote(hidden, xbuf.at[row_of(t)], ys_sem.at[d], yr_sem.at[d], c, tt)
        cp.start()
        y_copies.append(cp)
    first = remote(hidden, xbuf.at[row_of(t)], ps_sem.at[0], pr_sem.at[0], c, partner)
    first.start()

    @pl.when(has_next)
    def _():
        for tt in range(T):
            remote(hidden.at[pl.ds(r - PAD, PAD)], xbuf.at[pl.ds(0, PAD)],
                   hs_sem.at[tt], hr_sem, c + 1, tt).start()

    @pl.when(c == 0)
    def _():
        xbuf[pl.ds(0, PAD), :] = jnp.zeros((PAD, D), BF16)

    sw_pad[...] = jnp.zeros(sw_pad.shape, BF16)
    sw_pad[pl.ds(0, heads), :] = step_w[...]
    rows_pad[...] = jnp.zeros(rows_pad.shape, F32)
    rows_pad[pl.ds(0, 1), pl.ds(0, heads)] = step_bias[...]
    rows_pad[pl.ds(1, 1), pl.ds(0, heads)] = log_rate[...]
    rows_pad[pl.ds(2, 1), pl.ds(0, heads)] = skip_weight[...]

    forwards = []
    for d in range(1, Y):
        src = ((y + Y - d) % Y) * 2 + core
        y_copies[d - 1].wait_recv()
        cp = remote(xbuf.at[row_of(src)], xbuf.at[row_of(src)], ps_sem.at[d], pr_sem.at[d], c, partner)
        cp.start()
        forwards.append(cp)
    own.wait()
    first.wait_recv()
    for cp in forwards:
        cp.wait_recv()

    @pl.when(c > 0)
    def _():
        remote(hidden.at[pl.ds(r - PAD, PAD)], xbuf.at[pl.ds(0, PAD)],
               hs_sem.at[0], hr_sem, c, t).wait_recv()

    for cp in gws:
        cp.wait()
    gw = jnp.concatenate(
        [gw_vm[k].reshape(m_dev * GROUPS, LANES) for k in range(D // LANES)], axis=1
    )
    mt = dot_nt(gw, xbuf[...]).astype(BF16)
    q = m_dev * GROUPS
    dst_row, src_row = iota((q, q), 0), iota((q, q), 1)
    order = (src_row == (dst_row % m_dev) * GROUPS + dst_row // m_dev).astype(F32).astype(BF16)
    mt = dot(order, mt).astype(BF16)
    map_send[...] = mt.reshape(map_send.shape)
    m_copies = []
    for d in range(1, T):
        tt = (t + d) % T
        cp = remote(map_send.at[tt // span], map_recv.at[t], ms_sem.at[d], mr_sem.at[d], c, tt)
        cp.start()
        m_copies.append(cp)
    map_recv[t] = map_send[group]

    step_raw = dot_nt(xbuf[pl.ds(PAD, R), :], sw_pad[...]).astype(BF16).astype(F32)
    step = softplus(step_raw + rows_pad[0:1, :])
    log_step = -jnp.exp(rows_pad[1:2, :]) * step
    lower = (iota((R, R), 0) >= iota((R, R), 1)).astype(F32)
    cum = lax.dot_general(
        lower, log_step, (((1,), (0,)), ((), ())),
        preferred_element_type=F32, precision=lax.Precision.HIGHEST,
    )
    cum_t = cum.T
    last = cum[R - 1 : R, :]
    own_decay = jnp.exp(jnp.broadcast_to(last, (8, LANES)))
    dec_buf[...] = own_decay
    d_copies = []
    for d in range(1, C):
        cc = (c + d) % C
        cp = remote(dec_buf, dec_recv.at[c], ds_sem.at[d], dr_sem.at[d], cc, t)
        cp.start()
        d_copies.append(cp)
    dec_recv[c] = own_decay
    spread_row = iota((2 * LANES, inner), 0) % LANES
    spread = (spread_row == iota((2 * LANES, inner), 1) // HEAD_DIM).astype(F32).astype(BF16)
    step_wide = dot(split_terms(step), spread)
    tail_wide = dot(split_terms(jnp.exp(jnp.minimum(last - cum, 0.0)) * step), spread)
    cum_wide = dot(split_terms(jnp.exp(cum)), spread)
    skip_wide = dot(split_terms(rows_pad[...]), spread)[2:3, :]

    sel_r, sel_c = iota((LANES, 2 * LANES), 0), iota((LANES, 2 * LANES), 1)
    even = (sel_c == 2 * sel_r).astype(F32).astype(BF16)
    odd = (sel_c == 2 * sel_r + 1).astype(F32).astype(BF16)
    M = R + PAD
    for k in range(D // LANES):
        piece = xbuf[:, pl.ds(k * LANES, LANES)]
        xeo[pl.ds(0, R), pl.ds(2 * k * LANES, 2 * LANES)] = dot(piece[PAD:], even).astype(BF16)
        xeo[pl.ds(R, M), pl.ds(2 * k * LANES, 2 * LANES)] = dot(piece, odd).astype(BF16)
    for n in range(inner // (2 * LANES)):
        ws[2 * n].wait()
        ws[2 * n + 1].wait()
        w = jnp.concatenate(
            [w_vm[2 * n].reshape(2 * D, LANES), w_vm[2 * n + 1].reshape(2 * D, LANES)], axis=1
        )
        z = dot(xeo[...], w).astype(BF16)
        sl = pl.ds(2 * n * LANES, 2 * LANES)
        gate_buf[:, sl] = z[:R]
        raw[...] = z[R:].astype(F32)
        acc = inner_bias[:, sl]
        for k in range(KERNEL):
            acc = acc + conv_inner[k : k + 1, sl] * raw[pl.ds(PAD - KERNEL + 1 + k, R), :]
        x_buf[:, sl] = silu(acc).astype(BF16)

    for cp in m_copies:
        cp.wait_recv()
    eye = (iota((M, M), 0) == iota((M, M), 1)).astype(F32).astype(BF16)
    map_raw[...] = dot_nt(eye, map_recv[...].reshape(2 * STATE, M))
    gsl = pl.ds(pl.multiple_of(group * 2 * STATE, 2 * STATE), 2 * STATE)
    acc = group_bias[:, gsl]
    for k in range(KERNEL):
        acc = acc + conv_group[k : k + 1, gsl] * map_raw[pl.ds(PAD - KERNEL + 1 + k, R), :]
    maps = silu(acc).astype(BF16)
    b_map = maps[:, :STATE]
    c_map = maps[:, STATE:]
    eye_b = (iota((STATE, STATE), 0) == iota((STATE, STATE), 1)).astype(F32).astype(BF16)
    b_t = dot_nt(eye_b, b_map).astype(BF16)

    x_float = x_buf[...].astype(F32)
    weighted = (x_float * tail_wide).astype(BF16)
    state = dot(b_t, weighted)
    st_send[...] = state.astype(BF16).reshape(st_send.shape)
    for d in range(1, C):
        cc = (c + d) % C

        def send_state(cc=cc, d=d):
            remote(st_send.at[cc // stride], st_recv.at[c], ss_sem.at[d], sr_sem.at[d], cc, t).start()

        if stride == 1:
            send_state()
        else:
            pl.when(cc % stride == 0)(send_state)
    mine = c // stride
    st_recv[c] = st_send[mine]
    xt_buf[...] = (x_float * step_wide).astype(BF16)

    def mixing(pairs):
        scores = dot_nt(c_map, b_map) * lower
        half = R // 2
        for p in pairs:
            sl = pl.ds(p * LANES, LANES)
            xt = xt_buf[:, sl]
            parts = []
            for h in (2 * p, 2 * p + 1):
                col = cum[:, h : h + 1]
                row = cum_t[h : h + 1, :]
                top = jnp.exp(jnp.minimum(col[:half] - row[:, :half], 0.0)) * scores[:half, :half]
                bot = jnp.exp(jnp.minimum(col[half:] - row, 0.0)) * scores[half:]
                parts.append(
                    jnp.concatenate(
                        [dot(top.astype(BF16), xt[:half]), dot(bot.astype(BF16), xt)], axis=0
                    )
                )
            lane = iota((R, LANES), 1)
            gated_buf[:, sl] = jnp.where(lane < HEAD_DIM, parts[0], parts[1])

    pairs = inner // LANES
    cut = pairs // 2
    mixing(range(cut))

    def prefix():
        for d in range(1, C):
            remote(st_send.at[0], st_recv.at[c], ss_sem.at[d], sr_sem.at[d], c, t).wait_recv()
        running = jnp.zeros((slice_rows, inner), F32)
        for k in range(C):
            start_out[k] = running.astype(BF16)
            decay = dot(split_terms(dec_recv[k]), spread)[0:1, :]
            running = running * decay + st_recv[k].astype(F32)
        for d in range(1, C):
            cc = (c + d) % C
            remote(start_out.at[cc], start_buf.at[mine], bs_sem.at[d], br_sem.at[d], cc, t).start()
        start_buf[mine] = start_out[c]

    for cp in d_copies:
        cp.wait_recv()
    if stride == 1:
        prefix()
    else:
        pl.when(c % stride == 0)(prefix)

    mixing(range(cut, pairs))

    for d in range(1, C):
        def wait_start(d=d):
            remote(start_out.at[0], start_buf.at[mine], bs_sem.at[d], br_sem.at[d], c, t).wait_recv()

        if stride == 1:
            wait_start()
        else:
            pl.when((c + C - d) % C % stride == 0)(wait_start)
    starts = start_buf[...].reshape(STATE, inner)
    squares = jnp.zeros((R, LANES), F32)
    for p in range(pairs):
        sl = slice(p * LANES, (p + 1) * LANES)
        carried = dot(c_map, starts[:, sl]) * cum_wide[:, sl]
        value = gated_buf[:, sl] + carried + skip_wide[:, sl] * x_buf[:, sl].astype(F32)
        value = value * silu(gate_buf[:, sl].astype(F32))
        gated_buf[:, sl] = value
        squares = squares + value * value
    total = jnp.sum(squares, axis=1, keepdims=True)
    if span > 1:
        sq_send[...] = jnp.broadcast_to(total, (R, LANES))
        sq_copies = []
        for d in range(1, span):
            tt = group * span + (t % span + d) % span
            cp = remote(sq_send, sq_recv.at[d], sqs_sem.at[d], sqr_sem.at[d], c, tt)
            cp.start()
            sq_copies.append(cp)
        for d in range(1, span):
            sq_copies[d - 1].wait_recv()
            total = total + sq_recv[d][:, 0:1]
    inverse = lax.rsqrt(total / (HEADS * HEAD_DIM // GROUPS) + 1e-05)
    normed = (gated_buf[...] * inverse * norm_gain[...]).astype(BF16)
    nbuf[...] = normed.reshape(T, r, inner)

    ow.wait()
    other = jnp.concatenate([nbuf[2 * j + (1 - core)] for j in range(Y)], axis=0)
    q1 = []
    for n in range(NC):
        rs_send1[n] = dot(other, ow_vm[:, pl.ds(n * cols, cols)]).astype(BF16)
        cp = remote(rs_send1.at[n], rs_recv1.at[n], q1s_sem.at[n], q1r_sem.at[n], c, partner)
        cp.start()
        q1.append(cp)
    same = jnp.concatenate([nbuf[2 * j + core] for j in range(Y)], axis=0)
    q2 = []
    for n in range(NC):
        part = dot(same, ow_vm[:, pl.ds(n * cols, cols)])
        q1[n].wait_recv()
        s_buf[n] = (part + rs_recv1[n].astype(F32)).reshape(Y, r, cols)
        for d in range(1, Y):
            yy = (y + d) % Y
            rs_send2[n, d] = s_buf[n, yy].astype(BF16)
            cp = remote(rs_send2.at[n, d], rs_recv2.at[n, d], q2s_sem.at[n, d], q2r_sem.at[n, d],
                        c, yy * 2 + core)
            cp.start()
            q2.append(cp)
    for n in range(NC):
        part = s_buf[n, y]
        for d in range(1, Y):
            q2[n * (Y - 1) + d - 1].wait_recv()
            part = part + rs_recv2[n, d].astype(F32)
        out[:, pl.ds(n * cols, cols)] = part.astype(BF16)

    for cp in y_copies + [first] + forwards + m_copies + d_copies + q1 + q2:
        cp.wait_send()
    if span > 1:
        for cp in sq_copies:
            cp.wait_send()

    @pl.when(has_next)
    def _():
        for tt in range(T):
            remote(hidden.at[pl.ds(r - PAD, PAD)], xbuf.at[pl.ds(0, PAD)],
                   hs_sem.at[tt], hr_sem, c + 1, tt).wait_send()

    for d in range(1, C):
        cc = (c + d) % C

        def sent_state(cc=cc, d=d):
            remote(st_send.at[cc // stride], st_recv.at[c], ss_sem.at[d], sr_sem.at[d], cc, t).wait_send()

        def sent_start(cc=cc, d=d):
            remote(start_out.at[cc], start_buf.at[mine], bs_sem.at[d], br_sem.at[d], cc, t).wait_send()

        if stride == 1:
            sent_state()
            sent_start()
        else:
            pl.when(cc % stride == 0)(sent_state)
            pl.when(c % stride == 0)(sent_start)


def body(sizes, hidden, in_weight, step_weight, group_weight, conv_inner, inner_bias, conv_group,
         group_bias, step_bias, log_rate, skip_weight, norm_gain, out_weight):
    C, T = sizes
    Y = T // 2
    r, D = hidden.shape
    R = r * T
    M = R + PAD
    inner = out_weight.shape[0]
    m_dev = group_weight.shape[0]
    NS = min(C, STATE // 16)
    NC = 4
    cols = D // NC
    span = T // GROUPS
    vm = pl.BlockSpec(memory_space=pltpu.VMEM)
    hbm = pl.BlockSpec(memory_space=pl.ANY)
    V = pltpu.VMEM
    S = pltpu.SemaphoreType.DMA
    scratch = [
        V((M, D), BF16),
        V((inner // LANES, D, 2, LANES), BF16),
        V((D // LANES, m_dev, GROUPS, LANES), BF16),
        V((inner, D), BF16),
        V((LANES, D), BF16),
        V((8, LANES), F32),
        V((R + M, 2 * D), BF16),
        V((M, 2 * LANES), F32),
        V((R, inner), BF16),
        V((GROUPS, m_dev, M), BF16),
        V((T, m_dev, M), BF16),
        V((M, 2 * STATE), F32),
        V((R, inner), BF16),
        V((NS, STATE // NS, inner), BF16),
        V((C, STATE // NS, inner), BF16),
        V((8, LANES), F32),
        V((C, 8, LANES), F32),
        V((C, STATE // NS, inner), BF16),
        V((NS, STATE // NS, inner), BF16),
        V((R, inner), BF16),
        V((R, inner), F32),
        V((T, r, inner), BF16),
        V((NC, Y * r, cols), BF16),
        V((NC, Y * r, cols), BF16),
        V((NC, Y, r, cols), F32),
        V((NC, Y, r, cols), BF16),
        V((NC, Y, r, cols), BF16),
        V((R, LANES), F32),
        V((span, R, LANES), F32),
        S((inner // LANES,)), S((D // LANES,)), S, S,
        S((Y,)), S((Y,)), S((Y,)), S((Y,)), S((T,)), S,
        S((T,)), S((T,)), S((C,)), S((C,)), S((C,)), S((C,)), S((C,)), S((C,)),
        S((NC,)), S((NC,)), S((NC, Y)), S((NC, Y)), S((span,)), S((span,)),
    ]
    return pl.pallas_call(
        functools.partial(kernel, sizes),
        out_shape=jax.ShapeDtypeStruct((r, D), BF16),
        in_specs=[hbm, hbm, vm, hbm, vm, vm, vm, vm, vm, vm, vm, vm, hbm],
        out_specs=vm,
        scratch_shapes=scratch,
        compiler_params=pltpu.CompilerParams(
            collective_id=0, has_side_effects=True, vmem_limit_bytes=56 * 1024 * 1024
        ),
        cost_estimate=pl.CostEstimate(flops=8 * R * D * inner, bytes_accessed=16 * D * inner // 2, transcendentals=0),
        name="ssd_block",
    )(
        hidden, in_weight, step_weight.T, group_weight, conv_inner, inner_bias[None, :], conv_group,
        group_bias[None, :], step_bias[None, :], log_rate[None, :], skip_weight[None, :],
        norm_gain[None, :], out_weight,
    )


def solution(mesh):
    sizes = (mesh.shape["ctx"], mesh.shape["tp"])
    placed = (
        P(("ctx", "tp"), None),
        P(None, None, "tp"),
        P(None, "tp"),
        P("tp", None, None),
        P(None, "tp"),
        P("tp"),
        P(),
        P(),
        P("tp"),
        P("tp"),
        P("tp"),
        P("tp"),
        P("tp", None),
    )
    return jax.shard_map(
        functools.partial(body, sizes), mesh=mesh, in_specs=placed,
        out_specs=P(("ctx", "tp"), None), check_vma=False,
    )
```

time: 215 us -> 57.9 us (0.27)
  waiting for transfers between devices: 109 us -> 0 us
  Pallas kernels: 0 us -> 55.5 us
  blocking collectives: 26.5 us -> 0 us
  matrix products: 20.4 us -> 0 us
  local copies, waits for them, and re-layouts: 21.1 us -> 1.67 us
  other arithmetic: 16.1 us -> 0 us
  between operations: 13.5 us -> 0.01 us
  starting transfers between devices: 7.41 us -> 0 us
    all_gather x3 -> x0, waiting for transfers between devices: 78.3 us -> none  [the longest x1 51.1 us: entering(): everything = jax.tree.map(lambda part: lax.all_gather(part, axis), x)]
    pallas_call x0 -> x1, Pallas kernels: none -> 55.5 us  [body(): pl.pallas_call(functools.partial(kernel, sizes), out_shape=jax.ShapeDtype...]
    reduce_scatter x1 -> x0, waiting for transfers between devices: 30.1 us -> none  [body(): lax.psum_scatter(jnp.dot(normed, out_weight, preferred_element_type=jnp.f...]
    all_gather x1 -> x0, blocking collectives: 20.9 us -> none  [entering(): everything = jax.tree.map(lambda part: lax.all_gather(part, axis), x)]
    dot_general x8 -> x0, matrix products: 20.4 us -> none  [the longest x1 6.05 us: body(): jnp.dot(shard_rows, zx_weight, preferred_element_type=jnp.float32)]
    unnamed x24 -> x1, local copies, waits for them, and re-layouts: 13 us -> 1.67 us
    select_n x9 -> x0, other arithmetic: 9.46 us -> none  [the longest x8 9.38 us: turn(): return jax.tree.map(lambda a, b: jnp.where(reached, a, b), new, before)]
    ppermute x2 -> x0, starting transfers between devices: 7.29 us -> none  [shifted(): return lax.ppermute(x, axis, pairs)]
  transfers between devices with their start and end apart: 6 -> 0, of which waited for: 4 -> 0; matrix products, arithmetic and copies ran while one was open for 14% -> 0% of each run, Pallas kernels for 0% -> 0%
where the time goes in v1:
time: 57.9 us; the launch traced here: 57.2 us
  Pallas kernels  55.5 us (96%)
  local copies, waits for them, and re-layouts  1.67 us (3%)
    pallas_call x1, Pallas kernels, body(): pl.pallas_call(functools.partial(kernel, sizes), out_shape=jax.ShapeDtype...  55.5 us
    unnamed x1, local copies, waits for them, and re-layouts  1.67 us

profile of v1, /device:TPU:0, one launch (start us, length us, event | category | flops | bytes accessed | tf_op | source)
XLA Modules:
  0.0 57.2 jit_solution(15455494944215260606)
XLA Ops:
  0.0 55.5 %ssd_block.1 = bf16[64,2048]{1,0:T(8,128)(2,1)} custom-call(bf16[64,2048]{1,0:T(8,128)(2,1)} %hidden.1, bf16[2048,2,1024]{2,1,0:T(2,128)(2,1)} %in_w.1, bf16[16,2048]{1,0:T(8,128)(2,1)} %bitcast.7, bf16[64,4,2048]{2,1,0:T(4,128)(2,1)} %group_w.1, f32[4,1024]{1,0:T(4,128)} %conv_inner.1, f32[1,1024]{1,0:T(1,128)} %bitcast.8, f32[4,1024]{1,0:T(4,128)} %conv_group.1, ...), custom_call_target="tpu_custom_call" | custom-call | flops 4294967296 | bytes 16777216 | tf_op jit(solution)/shard_map/ssd_block/pallas_call | solution.py:460
  55.5 1.7 %copy.15 = bf16[64,2048]{1,0:T(8,128)(2,1)} copy(bf16[64,2048]{1,0:T(8,128)(2,1)} %ssd_block.1) | data formatting | bytes 524288
